TPU v7x, 256 devices: a whole 4x4x8 slice. The times are simulated.
256 devices in a mesh: blocks: 64 (over z, x, core), section: 4 (over y).
Axes of the slice: x: 4, y: 4, z: 8, core: 2. Of those that a mesh axis runs over, the one named last changes fastest.
Arguments:
- features: bfloat16 [256, 32, 4096], P(('blocks', 'section')), may hold values from -6 to 6
- grad_pool: bfloat16 [256, 32, 4096], P(('blocks', 'section')), may hold values from -6 to 6
- grad_skip: bfloat16 [256, 32, 4096], P(('blocks', 'section')), may hold values from -6 to 6
- conv_one: bfloat16 [27, 32, 32], replicated, may hold values from -0.21875 to 0.21875
- conv_two: bfloat16 [27, 32, 32], replicated, may hold values from -0.21875 to 0.21875
- block_links: int32 [256, 6], P(('blocks', 'section')), may hold values from -1 to 255, as said below
- block_positions: int32 [256, 3], P(('blocks', 'section')), may hold values from 0 to 4095
- dropout_seed: int32 [1], replicated, may hold values from 0 to 1048575
Outputs:
- encoded: bfloat16 [256, 32, 4096], P(('blocks', 'section'))
- grad_features: bfloat16 [256, 32, 4096], P(('blocks', 'section'))
- grad_conv_one: float32 [27, 32, 32], replicated
- grad_conv_two: float32 [27, 32, 32], replicated
Inputs may be any that keep to these rules, and one draw needn't show every extreme that they name: `block_links`: links are mutual: if entry 2k+1 (the + face along axis k) of block a is b, then entry 2k of block b is a, and the reverse. A block never names itself, and every block named is held by the same device as the naming block or by the device one index before or after it along blocks+section, the last and the first device counting as neighbours.
All inputs are finite; a program needn't handle non-finite values.
Results may differ from a plain program's by a relative error of at most 0.0059.
Values may be sent and summed in bfloat16 or wider, within the bound.
A program may use at most 192 MiB of HBM per device.

v0:
```python
import math
import jax
import jax.numpy as jnp
import numpy as np
from jax import lax
from jax.sharding import PartitionSpec as P

C = 32
EDGE = 16
keep_factor = 1024.0 / 819.0


def from_behind(block, axis, distance):
    devices = range(lax.axis_size(axis))
    route = [((i - distance) % len(devices), i) for i in devices]
    return lax.ppermute(block, axis, route)


def flat_faces(field):
    number = field.shape[0]
    plane = EDGE * EDGE
    volume = EDGE**3
    slabs = field.reshape(number, C, EDGE, plane)
    minus_x = field[:, :, :plane]
    plus_x = field[:, :, volume - plane :]
    minus_y = slabs[:, :, :, :EDGE].reshape(number, C, plane)
    plus_y = slabs[:, :, :, plane - EDGE :].reshape(number, C, plane)
    minus_z = field[:, :, 0::EDGE]
    plus_z = field[:, :, EDGE - 1 :: EDGE]
    return jnp.stack([minus_x, plus_x, minus_y, plus_y, minus_z, plus_z], axis=1)


def local_rims(local_layers, from_prev, from_next, block_links, my_index, device_count):
    per_device = local_layers.shape[0]
    face_pool = jnp.concatenate([from_prev, local_layers, from_next], axis=0)
    opposite = jnp.bitwise_xor(jnp.arange(6, dtype=jnp.int32), 1)[None, :]
    owner_device = block_links // per_device
    index_gap = (owner_device - my_index) % device_count
    source_slot = jnp.where(index_gap == 0, 1, jnp.where(index_gap == 1, 2, 0))
    pool_row = jnp.where(block_links >= 0, source_slot * per_device + block_links % per_device, 0)
    picked = face_pool[pool_row, opposite]
    return jnp.where((block_links >= 0)[:, :, None, None], picked, jnp.zeros_like(picked))


def spread_rims(rims):
    number = rims.shape[0]
    volume = EDGE**3
    spread_x = [jnp.tile(rims[:, face], (1, 1, EDGE)) for face in (0, 1)]
    spread_y = [
        jnp.tile(rims[:, face].reshape(number, C, EDGE, EDGE), (1, 1, 1, EDGE)).reshape(
            number, C, volume
        )
        for face in (2, 3)
    ]
    spread_z = [jnp.repeat(rims[:, face], EDGE, axis=2) for face in (4, 5)]
    return spread_x + spread_y + spread_z


def sliding_flattened(field, amount):
    volume = field.shape[-1]
    if amount == 0:
        return field
    pad_shape = field.shape[:-1] + (abs(amount),)
    zeros_pad = jnp.zeros(pad_shape, field.dtype)
    if amount > 0:
        return jnp.concatenate([field[..., amount:], zeros_pad], axis=-1)
    return jnp.concatenate([zeros_pad, field[..., : volume + amount]], axis=-1)


def offset_tables():
    plane = EDGE * EDGE
    volume = EDGE**3
    ruler = np.arange(volume)
    places = [ruler // plane, ruler // EDGE % EDGE, ruler % EDGE]
    strides = [plane, EDGE, 1]
    tables = []
    for offset in range(27):
        steps = [offset // 9 - 1, offset // 3 % 3 - 1, offset % 3 - 1]
        moved = steps[0] * plane + steps[1] * EDGE + steps[2]
        fits = [
            (places[axis_id] + steps[axis_id] >= 0) & (places[axis_id] + steps[axis_id] < EDGE)
            for axis_id in range(3)
        ]
        inside = fits[0] & fits[1] & fits[2]
        faces = []
        for axis_id in range(3):
            if steps[axis_id] != 0:
                others = [fits[other] for other in range(3) if other != axis_id]
                chosen = ~fits[axis_id] & others[0] & others[1]
                face = 2 * axis_id + (1 if steps[axis_id] > 0 else 0)
                faces.append((face, chosen, moved - steps[axis_id] * strides[axis_id]))
        tables.append((moved, inside, faces))
    return tables


def window_of(field, spread, table):
    moved, inside, faces = table
    result = jnp.where(
        jnp.asarray(inside)[None, None, :],
        sliding_flattened(field, moved),
        jnp.zeros((), field.dtype),
    )
    for face, chosen, amount in faces:
        result = jnp.where(
            jnp.asarray(chosen)[None, None, :], sliding_flattened(spread[face], amount), result
        )
    return result


def convolve(field, spread, kernel, incoming_gradient):
    number = field.shape[0]
    tables = offset_tables()
    summed = None
    pieces = []
    for group in range(3):
        stacked_tiles = jnp.stack(
            [
                window_of(field, spread, tables[offset])
                for offset in range(9 * group, 9 * group + 9)
            ],
            axis=1,
        )
        stacked_tiles = stacked_tiles.reshape(number, 9 * C, EDGE**3)
        if kernel is not None:
            weight_matrix = jnp.transpose(kernel[9 * group : 9 * group + 9], (1, 0, 2)).reshape(
                C, 9 * C
            )
            partial_value = jnp.einsum(
                "cr,xrq->xcq", weight_matrix, stacked_tiles, preferred_element_type=jnp.float32
            )
            summed = partial_value if summed is None else summed + partial_value
        if incoming_gradient is not None:
            product = jnp.einsum(
                "lfj,lpj->fp", incoming_gradient, stacked_tiles, preferred_element_type=jnp.float32
            )
            pieces.append(jnp.transpose(product.reshape(C, 9, C), (1, 0, 2)))
    grads = jnp.concatenate(pieces, axis=0) if incoming_gradient is not None else None
    return (summed, grads)


def mirrored_kernel(kernel):
    return jnp.transpose(kernel[::-1], (0, 2, 1))


def keep_scale(block_positions, dropout_seed):
    plane = EDGE * EDGE
    ruler = jnp.arange(EDGE**3, dtype=jnp.int32)
    global_x = block_positions[:, 0][:, None, None] * EDGE + (ruler // plane)[None, None, :]
    global_y = block_positions[:, 1][:, None, None] * EDGE + (ruler // EDGE % EDGE)[None, None, :]
    global_z = block_positions[:, 2][:, None, None] * EDGE + (ruler % EDGE)[None, None, :]
    channel = jnp.arange(C, dtype=jnp.int32)[None, :, None]
    hashed = jnp.bitwise_xor(global_x * jnp.int32(73856093), global_y * jnp.int32(19349663))
    hashed = jnp.bitwise_xor(hashed, global_z * jnp.int32(83492791))
    hashed = jnp.bitwise_xor(hashed, channel * jnp.int32(1103515245))
    hashed = jnp.bitwise_xor(hashed, dropout_seed[0] * jnp.int32(668265263))
    hashed = jnp.bitwise_xor(hashed, lax.shift_right_logical(hashed, jnp.int32(13)))
    hashed = hashed * jnp.int32(1274126177)
    hashed = jnp.bitwise_xor(hashed, lax.shift_right_logical(hashed, jnp.int32(16)))
    kept_mask = jnp.bitwise_and(hashed, jnp.int32(1023)) >= 205
    return jnp.where(kept_mask, jnp.float32(keep_factor), jnp.float32(0.0))


def trade_faces(layers):
    from_prev = from_behind(layers, ("blocks", "section"), 1)
    from_next = from_behind(layers, ("blocks", "section"), -1)
    return (from_prev, from_next)


def local(
    features, grad_pool, grad_skip, conv_one, conv_two, block_links, block_positions, dropout_seed
):
    device_count = lax.axis_size(("blocks", "section"))
    my_index = lax.axis_index(("blocks", "section"))
    per_device = features.shape[0]
    norm_factor = 1.0 / math.sqrt(per_device * device_count * EDGE**3)
    input_layers = flat_faces(features)
    upstream = (grad_pool.astype(jnp.float32) + grad_skip.astype(jnp.float32)).astype(jnp.bfloat16)
    in_prev, in_next = trade_faces(input_layers)
    spread_in = spread_rims(
        local_rims(input_layers, in_prev, in_next, block_links, my_index, device_count)
    )
    pre, unused_one = convolve(features, spread_in, conv_one, None)
    keep = keep_scale(block_positions, dropout_seed)
    dropped = (jax.nn.silu(pre) * keep).astype(jnp.bfloat16)
    dropped_layers = flat_faces(dropped)
    drop_prev, drop_next = trade_faces(dropped_layers)
    spread_drop = spread_rims(
        local_rims(dropped_layers, drop_prev, drop_next, block_links, my_index, device_count)
    )
    encoded_sum, partial_two = convolve(dropped, spread_drop, conv_two, upstream)
    encoded = encoded_sum.astype(jnp.bfloat16)
    partial_two = partial_two * norm_factor
    upstream_layers = flat_faces(upstream)
    up_prev, up_next = trade_faces(upstream_layers)
    upward_spread = spread_rims(
        local_rims(upstream_layers, up_prev, up_next, block_links, my_index, device_count)
    )
    back, unused_two = convolve(upstream, upward_spread, mirrored_kernel(conv_two), None)
    logistic = jax.nn.sigmoid(pre)
    inner = (back * keep * logistic * (1.0 + pre * (1.0 - logistic))).astype(jnp.bfloat16)
    unused_three, partial_one = convolve(features, spread_in, None, inner)
    partial_one = partial_one * norm_factor
    grad_conv_one, grad_conv_two = lax.psum((partial_one, partial_two), ("blocks", "section"))
    inner_layers = flat_faces(inner)
    inner_prev, inner_next = trade_faces(inner_layers)
    spread_inner = spread_rims(
        local_rims(inner_layers, inner_prev, inner_next, block_links, my_index, device_count)
    )
    grad_sum, unused_four = convolve(inner, spread_inner, mirrored_kernel(conv_one), None)
    grad_features = grad_sum.astype(jnp.bfloat16)
    return (encoded, grad_features, grad_conv_one, grad_conv_two)


def solution(mesh):
    in_specs = (
        P(("blocks", "section"), None, None),
        P(("blocks", "section"), None, None),
        P(("blocks", "section"), None, None),
        P(),
        P(),
        P(("blocks", "section"), None),
        P(("blocks", "section"), None),
        P(),
    )
    out_specs = (
        P(("blocks", "section"), None, None),
        P(("blocks", "section"), None, None),
        P(),
        P(),
    )
    return jax.shard_map(local, mesh=mesh, in_specs=in_specs, out_specs=out_specs, check_vma=False)
```

profile of v0, /device:TPU:1, one launch (start us, length us, event | category | flops | bytes accessed | tf_op | source)
XLA Modules:
  0.0 552.4 jit_solution(3824552230405607602)
XLA Ops:
  10.3 2.2 collective-permute-start.4
  12.5 2.1 collective-permute-start.5
  16.7 3.1 collective-permute-start.1
  75.3 1.5 copy.705
  88.5 1.5 copy.617
  93.0 1.9 copy.711
  114.6 1.7 constant_dynamic-update-slice_fusion.74
  129.7 1.6 fusion.40
  138.6 3.0 collective-permute-start.3
  141.6 2.2 fusion.225
  143.8 1.6 convolution_add_fusion.3
  153.7 3.3 collective-permute-start.7
  179.6 1.8 fusion.28
  181.4 1.8 fusion.25
  183.2 1.8 fusion.22
  203.0 1.5 copy.653
  207.4 1.5 copy.744
  254.4 1.8 fusion.37
  261.1 1.8 fusion.34
  270.0 1.8 fusion.31
  273.0 2.4 fusion.226
  281.9 259.8 %all-reduce.299.cloned.1.call-done = (f32[27,32,32]{2,1,0:T(8,128)}, f32[27,32,32]{2,1,0:T(8,128)}) async-done(((f32[27,32,32]{2,1,0:T(8,128)}, f32[27,32,32]{2,1,0:T(8,128)}), (f32[27,32,32]{2,1,0:T(8,128)}, f32[27,32,32]{2,1,0:T(8,128)})) %all-reduce.299.cloned.1.call-update) | async-done | bytes 221200 | tf_op jit(solution)/shard_map/psum | solution.py:203
  541.7 1.8 copy.906
  543.5 1.8 copy.907
  (1309 shorter events, 223.0 us)
Async XLA Ops:
  7.2 7.5 %copy-start = (bf16[1,32,4096]{2,1,0:T(8,128)(2,1)S(1)}, bf16[1,32,4096]{2,1,0:T(8,128)(2,1)}, u32[]{:S(2)}) copy-start(bf16[1,32,4096]{2,1,0:T(8,128)(2,1)} %param.413) | copy-start | bytes 786436
  7.2 534.5 %all-reduce.299.cloned.1.call-start = ((), (), s32[]{:S(2)}) async-start(), calls=%async_computation | async-start | bytes 1769472 | tf_op jit(solution)/shard_map/psum | solution.py:203
  10.3 41.2 %collective-permute-start.4 = (bf16[1,6,32,256]{3,2,1,0:T(8,128)(2,1)S(1)}, bf16[1,6,32,256]{3,2,1,0:T(8,128)(2,1)S(1)}, u32[]{:S(2)}, u32[]{:S(2)}) collective-permute-start(bf16[1,6,32,256]{3,2,1,0:T(8,128)(2,1)S(1)} %constant_dynamic-update-slice_fusion.66), channel_id=1, source_target_pairs={{255,0},{0,1},{1,2},{2,3},{3,4},{4,5},{5,6},{6,7},{7,8},{8,9},{9,1... | collective-permute-start | bytes 294920 | tf_op jit(solution)/shard_map/ppermute | solution.py:16
  12.5 39.0 %collective-permute-start.5 = (bf16[1,6,32,256]{3,2,1,0:T(8,128)(2,1)S(1)}, bf16[1,6,32,256]{3,2,1,0:T(8,128)(2,1)S(1)}, u32[]{:S(2)}, u32[]{:S(2)}) collective-permute-start(bf16[1,6,32,256]{3,2,1,0:T(8,128)(2,1)S(1)} %constant_dynamic-update-slice_fusion.66), channel_id=1, source_target_pairs={{1,0},{2,1},{3,2},{4,3},{5,4},{6,5},{7,6},{8,7},{9,8},{10,9},{11,1... | collective-permute-start | bytes 294920 | tf_op jit(solution)/shard_map/ppermute | solution.py:16
  16.6 35.6 %collective-permute-start = (bf16[1,6,32,256]{3,2,1,0:T(8,128)(2,1)S(1)}, bf16[1,6,32,256]{3,2,1,0:T(8,128)(2,1)S(1)}, u32[]{:S(2)}, u32[]{:S(2)}) collective-permute-start(bf16[1,6,32,256]{3,2,1,0:T(8,128)(2,1)S(1)} %constant_dynamic-update-slice_fusion), channel_id=1, source_target_pairs={{255,0},{0,1},{1,2},{2,3},{3,4},{4,5},{5,6},{6,7},{7,8},{8,9},{9,1... | collective-permute-start | bytes 294920 | tf_op jit(solution)/shard_map/ppermute | solution.py:16
  16.7 35.5 %collective-permute-start.1 = (bf16[1,6,32,256]{3,2,1,0:T(8,128)(2,1)S(1)}, bf16[1,6,32,256]{3,2,1,0:T(8,128)(2,1)S(1)}, u32[]{:S(2)}, u32[]{:S(2)}) collective-permute-start(bf16[1,6,32,256]{3,2,1,0:T(8,128)(2,1)S(1)} %constant_dynamic-update-slice_fusion), channel_id=1, source_target_pairs={{1,0},{2,1},{3,2},{4,3},{5,4},{6,5},{7,6},{8,7},{9,8},{10,9},{11,1... | collective-permute-start | bytes 294920 | tf_op jit(solution)/shard_map/ppermute | solution.py:16
  38.0 4.4 copy-start.297
  38.9 3.5 copy-start.298
  39.8 4.2 copy-start.468
  60.5 8.2 %copy-start.5 = (bf16[1,32,4096]{2,1,0:T(8,128)(2,1)}, bf16[1,32,4096]{2,1,0:T(8,128)(2,1)S(1)}, u32[]{:S(2)}) copy-start(bf16[1,32,4096]{2,1,0:T(8,128)(2,1)S(1)} %copy.608) | copy-start | bytes 786436
  117.9 3.1 copy-start.11
  117.9 3.1 copy-start.20
  136.1 7.7 %copy-start.24 = (bf16[1,9,32,4096]{3,2,1,0:T(8,128)(2,1)S(1)}, bf16[1,9,32,4096]{3,2,1,0:T(8,128)(2,1)}, u32[]{:S(2)}) copy-start(bf16[1,9,32,4096]{3,2,1,0:T(8,128)(2,1)} %copy-done.23) | copy-start | bytes 7077892
  138.6 47.3 %collective-permute-start.2 = (bf16[1,6,32,256]{3,2,1,0:T(8,128)(2,1)}, bf16[1,6,32,256]{3,2,1,0:T(8,128)(2,1)}, u32[]{:S(2)}, u32[]{:S(2)}) collective-permute-start(bf16[1,6,32,256]{3,2,1,0:T(8,128)(2,1)} %constant_dynamic-update-slice_fusion.33), channel_id=1, source_target_pairs={{255,0},{0,1},{1,2},{2,3},{3,4},{4,5},{5,6},{6,7},{7,8},{8,9},{9,1... | collective-permute-start | bytes 294920 | tf_op jit(solution)/shard_map/ppermute | solution.py:16
  138.6 47.3 %collective-permute-start.3 = (bf16[1,6,32,256]{3,2,1,0:T(8,128)(2,1)}, bf16[1,6,32,256]{3,2,1,0:T(8,128)(2,1)}, u32[]{:S(2)}, u32[]{:S(2)}) collective-permute-start(bf16[1,6,32,256]{3,2,1,0:T(8,128)(2,1)} %constant_dynamic-update-slice_fusion.33), channel_id=1, source_target_pairs={{1,0},{2,1},{3,2},{4,3},{5,4},{6,5},{7,6},{8,7},{9,8},{10,9},{11,1... | collective-permute-start | bytes 294920 | tf_op jit(solution)/shard_map/ppermute | solution.py:16
  153.7 33.8 %collective-permute-start.6 = (bf16[1,6,32,256]{3,2,1,0:T(8,128)(2,1)}, bf16[1,6,32,256]{3,2,1,0:T(8,128)(2,1)}, u32[]{:S(2)}, u32[]{:S(2)}) collective-permute-start(bf16[1,6,32,256]{3,2,1,0:T(8,128)(2,1)} %constant_dynamic-update-slice_fusion.99), channel_id=1, source_target_pairs={{255,0},{0,1},{1,2},{2,3},{3,4},{4,5},{5,6},{6,7},{7,8},{8,9},{9,1... | collective-permute-start | bytes 294920 | tf_op jit(solution)/shard_map/ppermute | solution.py:16
  153.7 33.8 %collective-permute-start.7 = (bf16[1,6,32,256]{3,2,1,0:T(8,128)(2,1)}, bf16[1,6,32,256]{3,2,1,0:T(8,128)(2,1)}, u32[]{:S(2)}, u32[]{:S(2)}) collective-permute-start(bf16[1,6,32,256]{3,2,1,0:T(8,128)(2,1)} %constant_dynamic-update-slice_fusion.99), channel_id=1, source_target_pairs={{1,0},{2,1},{3,2},{4,3},{5,4},{6,5},{7,6},{8,7},{9,8},{10,9},{11,1... | collective-permute-start | bytes 294920 | tf_op jit(solution)/shard_map/ppermute | solution.py:16
  177.8 3.5 copy-start.16
  179.6 3.6 copy-start.12
  197.4 4.4 copy-start.308
  219.7 20.5 %copy-start.3 = (bf16[1,32,4096]{2,1,0:T(8,128)(2,1)}, bf16[1,32,4096]{2,1,0:T(8,128)(2,1)S(1)}, u32[]{:S(2)}) copy-start(bf16[1,32,4096]{2,1,0:T(8,128)(2,1)S(1)} %copy.749) | copy-start | bytes 786436
  230.6 11.4 %copy-start.1 = (bf16[1,32,4096]{2,1,0:T(8,128)(2,1)}, bf16[1,32,4096]{2,1,0:T(8,128)(2,1)S(1)}, u32[]{:S(2)}) copy-start(bf16[1,32,4096]{2,1,0:T(8,128)(2,1)S(1)} %copy.755) | copy-start | bytes 786436
  261.0 3.1 copy-start.261
  272.1 3.3 copy-start.303
  (456 other events, 820.4 us)
Sparse Core Ops, SparseCore 0:
  273.1 268.5 all-reduce.298
where the time goes:
time: 559 us; the launch traced here: 552 us
  waiting for transfers between devices  260 us (47%)
  local copies, waits for them, and re-layouts  200 us (36%)
  other arithmetic  30 us (5%)
  matrix products  24.9 us (4%)
  between operations  24 us (4%)
  starting transfers between devices  13.8 us (2%)
    psum x1, waiting for transfers between devices, local(): lax.psum((partial_one, partial_two), ('blocks', 'section'))  260 us
    slice x148, local copies, waits for them, and re-layouts, sliding_flattened(): return jnp.concatenate([field[..., amount:], zeros_pad], axis=-1)  120 us
    unnamed x968, local copies, waits for them, and re-layouts  22.6 us
    unnamed x46, other arithmetic  21.9 us
    broadcast_in_dim x16, local copies, waits for them, and re-layouts, spread_rims(): spread_z = [jnp.repeat(rims[:, face], EDGE, axis=2) for face in (4, 5)]  16.8 us
    dot_general x12, matrix products, convolve(): jnp.einsum('cr,xrq->xcq', weight_matrix, stacked_tiles, preferred_element...  14.2 us
    ppermute x8, starting transfers between devices, from_behind(): return lax.ppermute(block, axis, route)  13.8 us
    another operation x16, local copies, waits for them, and re-layouts, spread_rims(): jnp.tile(rims[:, face].reshape(number, C, EDGE, EDGE), (1, 1, 1, EDGE))  12.8 us
  transfers between devices with their start and end apart: 9, of which 1 were waited for; matrix products, arithmetic and copies ran while one was open for 15% of the time, Pallas kernels for 0%

commit v1 on v0

--- a/solution.py
+++ b/solution.py
@@ -200,7 +200,9 @@
     inner = (back * keep * logistic * (1.0 + pre * (1.0 - logistic))).astype(jnp.bfloat16)
     unused_three, partial_one = convolve(features, spread_in, None, inner)
     partial_one = partial_one * norm_factor
-    grad_conv_one, grad_conv_two = lax.psum((partial_one, partial_two), ("blocks", "section"))
+    grad_conv_one, grad_conv_two = lax.psum(
+        lax.psum((partial_one, partial_two), "blocks"), "section"
+    )
     inner_layers = flat_faces(inner)
     inner_prev, inner_next = trade_faces(inner_layers)
     spread_inner = spread_rims(

time: 559 us -> 540 us (0.966)
  waiting for transfers between devices: 260 us -> 241 us
    psum x1 -> x2, waiting for transfers between devices: 260 us -> 241 us  [the longest x1 191 us: local(): lax.psum((partial_one, partial_two), 'blocks')]
  transfers between devices with their start and end apart: 9 -> 10, of which waited for: 1 -> 2; matrix products, arithmetic and copies ran while one was open for 15% -> 15% of each run, Pallas kernels for 0% -> 0%
where the time goes in v1:
time: 540 us; the launch traced here: 533 us
  waiting for transfers between devices  241 us (45%)
  local copies, waits for them, and re-layouts  199 us (37%)
  other arithmetic  30 us (6%)
  matrix products  25 us (5%)
  between operations  24 us (4%)
  starting transfers between devices  13.9 us (3%)
    psum x1, waiting for transfers between devices, local(): lax.psum((partial_one, partial_two), 'blocks')  191 us
    slice x148, local copies, waits for them, and re-layouts, sliding_flattened(): return jnp.concatenate([field[..., amount:], zeros_pad], axis=-1)  120 us
    psum x1, waiting for transfers between devices, local(): lax.psum(lax.psum((partial_one, partial_two), 'blocks'), 'section')  49.8 us
    unnamed x46, other arithmetic  21.9 us
    unnamed x968, local copies, waits for them, and re-layouts  21.9 us
    broadcast_in_dim x16, local copies, waits for them, and re-layouts, spread_rims(): spread_z = [jnp.repeat(rims[:, face], EDGE, axis=2) for face in (4, 5)]  16.7 us
    dot_general x12, matrix products, convolve(): jnp.einsum('cr,xrq->xcq', weight_matrix, stacked_tiles, preferred_element...  14.2 us
    ppermute x8, starting transfers between devices, from_behind(): return lax.ppermute(block, axis, route)  13.8 us
  transfers between devices with their start and end apart: 10, of which 2 were waited for; matrix products, arithmetic and copies ran while one was open for 15% of the time, Pallas kernels for 0%

profile of v1, /device:TPU:1, one launch (start us, length us, event | category | flops | bytes accessed | tf_op | source)
XLA Modules:
  0.0 532.9 jit_solution(15140092558446589369)
XLA Ops:
  10.3 2.2 collective-permute-start.4
  12.5 2.1 collective-permute-start.5
  16.7 3.1 collective-permute-start.1
  71.0 1.5 copy.611
  75.5 1.5 copy.705
  93.0 1.9 copy.711
  114.8 1.7 constant_dynamic-update-slice_fusion.74
  129.9 1.6 fusion.40
  138.7 3.0 collective-permute-start.3
  141.7 2.3 fusion.225
  144.0 1.6 convolution_add_fusion.3
  153.9 3.3 collective-permute-start.7
  179.8 1.8 fusion.28
  181.6 1.8 fusion.25
  183.4 1.8 fusion.22
  203.2 1.5 copy.653
  254.7 1.8 fusion.37
  261.4 1.8 fusion.34
  270.3 1.8 fusion.31
  273.3 2.4 fusion.226
  280.2 190.9 %all-reduce.301.cloned.1.call-done = (f32[27,32,32]{2,1,0:T(8,128)}, f32[27,32,32]{2,1,0:T(8,128)}) async-done(((f32[27,32,32]{2,1,0:T(8,128)}, f32[27,32,32]{2,1,0:T(8,128)}), (f32[27,32,32]{2,1,0:T(8,128)}, f32[27,32,32]{2,1,0:T(8,128)})) %all-reduce.301.cloned.1.call-update) | async-done | bytes 221200 | tf_op jit(solution)/shard_map/psum | solution.py:204
  472.5 49.8 %all-reduce.303.cloned.1.call-done = (f32[27,32,32]{2,1,0:T(8,128)}, f32[27,32,32]{2,1,0:T(8,128)}) async-done(((f32[27,32,32]{2,1,0:T(8,128)}, f32[27,32,32]{2,1,0:T(8,128)}), (f32[27,32,32]{2,1,0:T(8,128)}, f32[27,32,32]{2,1,0:T(8,128)})) %all-reduce.303.cloned.1.call-update) | async-done | bytes 221200 | tf_op jit(solution)/shard_map/psum | solution.py:203
  522.2 1.8 copy.908
  524.0 1.8 copy.909
  (1312 shorter events, 224.1 us)
Async XLA Ops:
  7.2 7.5 %copy-start = (bf16[1,32,4096]{2,1,0:T(8,128)(2,1)S(1)}, bf16[1,32,4096]{2,1,0:T(8,128)(2,1)}, u32[]{:S(2)}) copy-start(bf16[1,32,4096]{2,1,0:T(8,128)(2,1)} %param.413) | copy-start | bytes 786436
  7.2 463.9 %all-reduce.301.cloned.1.call-start = ((), (), s32[]{:S(2)}) async-start(), calls=%async_computation | async-start | bytes 1769472 | tf_op jit(solution)/shard_map/psum | solution.py:204
  10.3 41.3 %collective-permute-start.4 = (bf16[1,6,32,256]{3,2,1,0:T(8,128)(2,1)S(1)}, bf16[1,6,32,256]{3,2,1,0:T(8,128)(2,1)S(1)}, u32[]{:S(2)}, u32[]{:S(2)}) collective-permute-start(bf16[1,6,32,256]{3,2,1,0:T(8,128)(2,1)S(1)} %constant_dynamic-update-slice_fusion.66), channel_id=1, source_target_pairs={{255,0},{0,1},{1,2},{2,3},{3,4},{4,5},{5,6},{6,7},{7,8},{8,9},{9,1... | collective-permute-start | bytes 294920 | tf_op jit(solution)/shard_map/ppermute | solution.py:16
  12.5 39.1 %collective-permute-start.5 = (bf16[1,6,32,256]{3,2,1,0:T(8,128)(2,1)S(1)}, bf16[1,6,32,256]{3,2,1,0:T(8,128)(2,1)S(1)}, u32[]{:S(2)}, u32[]{:S(2)}) collective-permute-start(bf16[1,6,32,256]{3,2,1,0:T(8,128)(2,1)S(1)} %constant_dynamic-update-slice_fusion.66), channel_id=1, source_target_pairs={{1,0},{2,1},{3,2},{4,3},{5,4},{6,5},{7,6},{8,7},{9,8},{10,9},{11,1... | collective-permute-start | bytes 294920 | tf_op jit(solution)/shard_map/ppermute | solution.py:16
  16.6 35.7 %collective-permute-start = (bf16[1,6,32,256]{3,2,1,0:T(8,128)(2,1)S(1)}, bf16[1,6,32,256]{3,2,1,0:T(8,128)(2,1)S(1)}, u32[]{:S(2)}, u32[]{:S(2)}) collective-permute-start(bf16[1,6,32,256]{3,2,1,0:T(8,128)(2,1)S(1)} %constant_dynamic-update-slice_fusion), channel_id=1, source_target_pairs={{255,0},{0,1},{1,2},{2,3},{3,4},{4,5},{5,6},{6,7},{7,8},{8,9},{9,1... | collective-permute-start | bytes 294920 | tf_op jit(solution)/shard_map/ppermute | solution.py:16
  16.7 35.6 %collective-permute-start.1 = (bf16[1,6,32,256]{3,2,1,0:T(8,128)(2,1)S(1)}, bf16[1,6,32,256]{3,2,1,0:T(8,128)(2,1)S(1)}, u32[]{:S(2)}, u32[]{:S(2)}) collective-permute-start(bf16[1,6,32,256]{3,2,1,0:T(8,128)(2,1)S(1)} %constant_dynamic-update-slice_fusion), channel_id=1, source_target_pairs={{1,0},{2,1},{3,2},{4,3},{5,4},{6,5},{7,6},{8,7},{9,8},{10,9},{11,1... | collective-permute-start | bytes 294920 | tf_op jit(solution)/shard_map/ppermute | solution.py:16
  38.1 4.4 copy-start.297
  39.0 3.6 copy-start.298
  39.9 4.3 copy-start.468
  60.7 8.1 %copy-start.5 = (bf16[1,32,4096]{2,1,0:T(8,128)(2,1)}, bf16[1,32,4096]{2,1,0:T(8,128)(2,1)S(1)}, u32[]{:S(2)}) copy-start(bf16[1,32,4096]{2,1,0:T(8,128)(2,1)S(1)} %copy.608) | copy-start | bytes 786436
  136.3 7.7 %copy-start.24 = (bf16[1,9,32,4096]{3,2,1,0:T(8,128)(2,1)S(1)}, bf16[1,9,32,4096]{3,2,1,0:T(8,128)(2,1)}, u32[]{:S(2)}) copy-start(bf16[1,9,32,4096]{3,2,1,0:T(8,128)(2,1)} %copy-done.23) | copy-start | bytes 7077892
  138.7 47.4 %collective-permute-start.2 = (bf16[1,6,32,256]{3,2,1,0:T(8,128)(2,1)}, bf16[1,6,32,256]{3,2,1,0:T(8,128)(2,1)}, u32[]{:S(2)}, u32[]{:S(2)}) collective-permute-start(bf16[1,6,32,256]{3,2,1,0:T(8,128)(2,1)} %constant_dynamic-update-slice_fusion.33), channel_id=1, source_target_pairs={{255,0},{0,1},{1,2},{2,3},{3,4},{4,5},{5,6},{6,7},{7,8},{8,9},{9,1... | collective-permute-start | bytes 294920 | tf_op jit(solution)/shard_map/ppermute | solution.py:16
  138.7 47.4 %collective-permute-start.3 = (bf16[1,6,32,256]{3,2,1,0:T(8,128)(2,1)}, bf16[1,6,32,256]{3,2,1,0:T(8,128)(2,1)}, u32[]{:S(2)}, u32[]{:S(2)}) collective-permute-start(bf16[1,6,32,256]{3,2,1,0:T(8,128)(2,1)} %constant_dynamic-update-slice_fusion.33), channel_id=1, source_target_pairs={{1,0},{2,1},{3,2},{4,3},{5,4},{6,5},{7,6},{8,7},{9,8},{10,9},{11,1... | collective-permute-start | bytes 294920 | tf_op jit(solution)/shard_map/ppermute | solution.py:16
  153.9 33.8 %collective-permute-start.6 = (bf16[1,6,32,256]{3,2,1,0:T(8,128)(2,1)}, bf16[1,6,32,256]{3,2,1,0:T(8,128)(2,1)}, u32[]{:S(2)}, u32[]{:S(2)}) collective-permute-start(bf16[1,6,32,256]{3,2,1,0:T(8,128)(2,1)} %constant_dynamic-update-slice_fusion.99), channel_id=1, source_target_pairs={{255,0},{0,1},{1,2},{2,3},{3,4},{4,5},{5,6},{6,7},{7,8},{8,9},{9,1... | collective-permute-start | bytes 294920 | tf_op jit(solution)/shard_map/ppermute | solution.py:16
  153.9 33.9 %collective-permute-start.7 = (bf16[1,6,32,256]{3,2,1,0:T(8,128)(2,1)}, bf16[1,6,32,256]{3,2,1,0:T(8,128)(2,1)}, u32[]{:S(2)}, u32[]{:S(2)}) collective-permute-start(bf16[1,6,32,256]{3,2,1,0:T(8,128)(2,1)} %constant_dynamic-update-slice_fusion.99), channel_id=1, source_target_pairs={{1,0},{2,1},{3,2},{4,3},{5,4},{6,5},{7,6},{8,7},{9,8},{10,9},{11,1... | collective-permute-start | bytes 294920 | tf_op jit(solution)/shard_map/ppermute | solution.py:16
  178.0 3.5 copy-start.16
  179.8 3.6 copy-start.12
  197.6 4.4 copy-start.308
  219.9 20.5 %copy-start.3 = (bf16[1,32,4096]{2,1,0:T(8,128)(2,1)}, bf16[1,32,4096]{2,1,0:T(8,128)(2,1)S(1)}, u32[]{:S(2)}) copy-start(bf16[1,32,4096]{2,1,0:T(8,128)(2,1)S(1)} %copy.749) | copy-start | bytes 786436
  230.8 11.5 %copy-start.1 = (bf16[1,32,4096]{2,1,0:T(8,128)(2,1)}, bf16[1,32,4096]{2,1,0:T(8,128)(2,1)S(1)}, u32[]{:S(2)}) copy-start(bf16[1,32,4096]{2,1,0:T(8,128)(2,1)S(1)} %copy.755) | copy-start | bytes 786436
  272.4 3.3 copy-start.303
  273.3 249.0 %all-reduce.303.cloned.1.call-start = ((), (), s32[]{:S(2)}) async-start(), calls=%async_computation.1 | async-start | bytes 1769472 | tf_op jit(solution)/shard_map/psum | solution.py:203
  278.6 192.5 %copy-start.10 = (bf16[1,9,32,4096]{3,2,1,0:T(8,128)(2,1)S(1)}, bf16[1,9,32,4096]{3,2,1,0:T(8,128)(2,1)}, u32[]{:S(2)}) copy-start(bf16[1,9,32,4096]{3,2,1,0:T(8,128)(2,1)} %copy-done.9) | copy-start | bytes 7077892
  278.6 192.5 %copy-start.301 = (bf16[32,9,32]{0,2,1:T(8,128)(2,1)S(1)}, bf16[32,9,32]{0,2,1:T(8,128)(2,1)}, u32[]{:S(2)}) copy-start(bf16[32,9,32]{0,2,1:T(8,128)(2,1)} %copy.694) | copy-start | bytes 55300
  (457 other events, 825.8 us)
Sparse Core Ops, SparseCore 0:
  273.4 197.6 all-reduce.300
  473.6 48.5 all-reduce.302
